TPU v7x, 256 devices: a whole 4x4x8 slice. The times are simulated.
256 devices in a mesh: dp: 64 (over y, z, core), tensor: 4 (over x).
Axes of the slice: x: 4, y: 4, z: 8, core: 2. Of those that a mesh axis runs over, the one named last changes fastest.
Arguments:
- activations: bfloat16 [65536, 4096], P(('dp', 'tensor')), may hold values from -6 to 6
- cotangent: bfloat16 [2, 65536, 1024], P(None, 'dp', 'tensor'), may hold values from -0.19921875 to 0.19921875
- error_memory: bfloat16 [2, 64, 4096, 1024], P(None, 'dp', None, 'tensor'), may hold values from -3 to 3
- right_factor: float32 [2, 1024, 32], P(None, 'tensor'), may hold values from -6 to 6
Outputs:
- new_error: bfloat16 [2, 64, 4096, 1024], P(None, 'dp', None, 'tensor')
- left_factor: float32 [2, 4, 4096, 32], P(None, 'tensor')
- mean_right: float32 [2, 1024, 32], P(None, 'tensor')
All inputs are finite; a program needn't handle non-finite values.
Results may differ from a plain program's by a relative error of at most 0.00045.
Values may be sent and summed in bfloat16 or wider, within the bound.
A program may use at most 128 MiB of HBM per device.

v0:
```python
import functools

import jax
import jax.numpy as jnp
from jax import lax
from jax.experimental import pallas as pl
from jax.experimental.pallas import tpu as pltpu
from jax.sharding import PartitionSpec as P

MESH = pl.DeviceIdType.MESH
BF = jnp.bfloat16
F32 = jnp.float32
NX = 4
RANK = 32
NT = (((1,), (1,)), ((), ()))
TN = (((0,), (0,)), ((), ()))


def split(value):
    high = value.astype(BF)
    return high, (value - high.astype(F32)).astype(BF)


def dot(a, b, dims=None):
    if dims is None:
        dims = (((1,), (0,)), ((), ()))
    return lax.dot_general(a, b, dims, preferred_element_type=F32)


def inverse_factor(gram):
    rows = lax.broadcasted_iota(jnp.int32, (RANK, 2 * RANK), 0)
    cols = lax.broadcasted_iota(jnp.int32, (RANK, 2 * RANK), 1)
    eye = jnp.where(cols == rows + RANK, 1.0, 0.0).astype(F32)
    wide = jnp.concatenate([gram, jnp.zeros((RANK, RANK), F32)], axis=1) + eye
    index = rows[:, :1]
    pivots = jnp.ones((RANK, 1), F32)
    for j in range(RANK):
        row = wide[j:j + 1, :]
        pivot = wide[j:j + 1, j:j + 1]
        column = wide[:, j:j + 1]
        factor = jnp.where(index > j, column * (1.0 / pivot), 0.0)
        pivots = jnp.where(index == j, pivot, pivots)
        wide = wide - factor * row
    return wide[:, RANK:] * (1.0 / jnp.sqrt(pivots))


def fused(NY, NZ, a_hbm, c_hbm, e_hbm, rt_hbm, new_hbm, left_hbm, mean_ref,
          a, c, e, rt, v, vall, vl, rb, pe, p, rc, fy, ry, q, rz, sp, rx, s, sb, sf, us, uf, left, stack, mem, new,
          t, ta, t2, ty, tf,
          lsem, vs, vr, xs, xr, cs, cr, fs, fr, ys, yr, zs, zr, ws, wr, gzs, gzr, gys, gyr, ghs, ghr, gcs, gcr,
          us_sem, ur_sem, tas, tar, tys, tyr, tgs, tgr, out_sem):
    dp, x = lax.axis_index("dp"), lax.axis_index("tensor")
    core, yz = lax.rem(dp, 2), lax.div(dp, 2)
    z, y = lax.rem(yz, NZ), lax.div(yz, NZ)
    other = 1 - core
    tokens = a.shape[1]
    width = a.shape[2]
    kv = c.shape[2]
    span = NY * 128
    ndp = 2 * NY * NZ

    def at_x(k):
        return {"dp": dp, "tensor": lax.rem(x + k, NX)}

    def at_y(k):
        return {"dp": (lax.rem(y + k, NY) * NZ + z) * 2 + core, "tensor": x}

    def at_zc(zz, cc):
        return {"dp": (y * NZ + zz) * 2 + cc, "tensor": x}

    def at_z(zz):
        return at_zc(zz, core)

    partner = at_zc(z, other)
    plane = [(d, k) for d in range(2) for k in range(NZ) if d + k]

    def remote(src, dst, send, recv, device):
        return pltpu.make_async_remote_copy(src_ref=src, dst_ref=dst, send_sem=send, recv_sem=recv,
                                            device_id=device, device_id_type=MESH)

    load_a = pltpu.make_async_copy(a_hbm, a.at[x], lsem.at[0])
    load_c = pltpu.make_async_copy(c_hbm, c, lsem.at[1])
    load_e = pltpu.make_async_copy(e_hbm, e, lsem.at[2])
    load_r = pltpu.make_async_copy(rt_hbm, rt, lsem.at[3])
    load_r.start()
    load_c.start()

    barrier = pltpu.get_barrier_semaphore()
    for k in range(1, NX):
        pl.semaphore_signal(barrier, inc=1, device_id=at_x(k), device_id_type=MESH)
    for k in range(1, NY):
        pl.semaphore_signal(barrier, inc=1, device_id=at_y(k), device_id_type=MESH)
    for d, k in plane:
        pl.semaphore_signal(barrier, inc=1, device_id=at_zc(lax.rem(z + k, NZ), (core, other)[d]), device_id_type=MESH)

    load_r.wait()
    load_c.wait()
    load_a.start()
    load_e.start()
    for m in range(2):
        high, low = split(rt[m])
        rb[m] = jnp.concatenate([high, low], axis=0)
        both = dot(rb[m], c[m], NT)
        vt = both[:RANK] + both[RANK:]
        for b in range(NX):
            v[b, m * RANK:(m + 1) * RANK, :] = vt[:, b * tokens:(b + 1) * tokens]

    pl.semaphore_wait(barrier, NX + NY + 2 * NZ - 3)

    v_copies = []
    for k in range(1, NX):
        copy = remote(v.at[lax.rem(x + k, NX)], vall.at[x], vs.at[k - 1], vr.at[k - 1], at_x(k))
        copy.start()
        v_copies.append(copy)

    quarter = tokens // 4
    left_x, right_x = lax.rem(x + NX - 1, NX), lax.rem(x + 1, NX)
    far_x = lax.rem(x + 2, NX)
    right_dev, left_dev = at_x(1), at_x(NX - 1)

    def quarter_copy(slot, i, sem, device):
        part = a.at[slot, pl.ds(i * quarter, quarter)]
        return remote(part, part, xs.at[sem], xr.at[sem], device)

    def own_quarter(i, sem, device):
        part = pl.ds(i * quarter, quarter)
        return remote(a_hbm.at[part], a.at[x, part], xs.at[sem], xr.at[sem], device)

    to_right = [own_quarter(i, i, right_dev) for i in range(4)]
    to_left = [own_quarter(i, 4 + i, left_dev) for i in (2, 3, 0, 1)]
    forward_right = [quarter_copy(left_x, i, 8 + i, right_dev) for i in range(2)]
    forward_left = [quarter_copy(right_x, 2 + i, 10 + i, left_dev) for i in range(2)]
    for i in range(2):
        to_right[i].start()
        to_left[i].start()

    def left_arrived(parts):
        for i in parts:
            quarter_copy(left_x, i, i, right_dev).wait_recv()

    def right_arrived(parts):
        for i in parts:
            quarter_copy(right_x, i, 4 + i, right_dev).wait_recv()

    def far_arrived():
        for i in range(2):
            quarter_copy(far_x, i, 8 + i, right_dev).wait_recv()
            quarter_copy(far_x, 2 + i, 10 + i, right_dev).wait_recv()

    load_e.wait()
    load_a.wait()

    def error_part(j, carry):
        at = pl.ds(pl.multiple_of(j * span, span), span)
        for m in range(2):
            et = dot(rb[m], e[m, at, :], NT)
            et = et[:RANK] + et[RANK:]
            for yb in range(NY):
                pe[m, j, yb] = et[:, yb * 128:(yb + 1) * 128]
        return carry

    lax.fori_loop(0, NZ, error_part, 0)

    vall[x] = v[x]
    for k in range(1, NX):
        src = lax.rem(x + NX - k, NX)
        remote(v.at[0], vall.at[src], vs.at[k - 1], vr.at[k - 1], at_x(k)).wait_recv()
    stacked = jnp.concatenate(
        [vall[b, m * RANK:(m + 1) * RANK, :] for m in range(2) for b in range(NX)], axis=0)
    high, low = split(stacked)
    block = 2 * NX * RANK
    vl[:block] = high
    vl[block:] = low

    def partials(j):
        zj = lax.rem(z + 1 + j, NZ)
        at = pl.ds(pl.multiple_of(zj * span, span), span)
        both = dot(vl[...], a[x, :, at])
        both = both[:block] + both[block:]
        for m in range(2):
            for yb in range(NY):
                for b in range(NX):
                    r0 = (m * NX + b) * RANK
                    p[m, zj, yb, b] = both[r0:r0 + RANK, yb * 128:(yb + 1) * 128]
        for m in range(2):
            for yb in range(NY):
                p[m, zj, yb, x] = p[m, zj, yb, x] + pe[m, zj, yb]
        remote(p.at[other, zj], rc.at[zj], cs.at[zj], cr.at[zj], partner).start()

    hc = NX // 2
    up, down, far_y = lax.rem(y + 1, NY), lax.rem(y + NY - 1, NY), lax.rem(y + 2, NY)
    to_up, to_down = at_y(1), at_y(NY - 1)

    def over_cores(j):
        zj = lax.rem(z + 1 + j, NZ)
        remote(p.at[other, zj], rc.at[zj], cs.at[zj], cr.at[zj], partner).wait_recv()
        p[core, zj] = p[core, zj] + rc[zj]
        remote(p.at[core, zj, far_y, pl.ds(0, hc)], fy.at[0, zj], fs.at[0, zj], fr.at[0, zj], to_up).start()
        remote(p.at[core, zj, far_y, pl.ds(hc, hc)], fy.at[1, zj], fs.at[1, zj], fr.at[1, zj], to_down).start()

    def staggered(j, carry):
        partials(j)
        over_cores(j - 1)
        return carry

    partials(0)
    lax.fori_loop(1, NZ, staggered, 0)
    over_cores(NZ - 1)

    to_right[2].start()
    to_left[2].start()

    def to_neighbours(j, carry):
        zj = lax.rem(z + 1 + j, NZ)
        for i, target, device in ((0, up, to_up), (1, down, to_down)):
            part = pl.ds(i * hc, hc)
            remote(p.at[core, zj, far_y, part], fy.at[i, zj], fs.at[i, zj], fr.at[i, zj], device).wait_recv()
            p[core, zj, target, part] = p[core, zj, target, part] + fy[i, zj]
            remote(p.at[core, zj, target], ry.at[i, zj], ys.at[i, zj], yr.at[i, zj], device).start()
        return carry

    lax.fori_loop(0, NZ, to_neighbours, 0)

    step = min(512, width)

    def cotangents(parts):
        rows = [pl.ds(pl.multiple_of(slot * tokens + r0, n), n) for slot, r0, n in parts]
        return jnp.concatenate([jnp.concatenate([c[0, r, :], c[1, r, :]], axis=1) for r in rows], axis=0)

    def product(parts, cc, at):
        return dot(jnp.concatenate([a[slot, r0:r0 + n, at] for slot, r0, n in parts], axis=0), cc, TN)

    def accumulate(parts, first=False):
        cc = cotangents(parts)

        def body(i, carry):
            at = pl.ds(pl.multiple_of(i * step, step), step)
            g = product(parts, cc, at)
            for m in range(2):
                base = e[m, at, :].astype(F32) if first else mem[m, at, :]
                mem[m, at, :] = base + g[:, m * kv:(m + 1) * kv]
            return carry

        lax.fori_loop(0, width // step, body, 0)

    half = tokens // 2
    accumulate([(x, 0, tokens)], True)

    def over_y(zj):
        total = p[core, zj, y]
        for i in range(2):
            remote(p.at[core, zj, y], ry.at[i, zj], ys.at[i, zj], yr.at[i, zj], partner).wait_recv()
            total = total + ry[i, zj]
        q[zj] = total

    def over_y_send(j, carry):
        zj = lax.rem(z + 1 + j, NZ)
        over_y(zj)
        remote(q.at[zj], rz.at[j], zs.at[j], zr.at[j], at_z(zj)).start()
        return carry

    lax.fori_loop(0, NZ - 1, over_y_send, 0)
    over_y(z)

    total = q[z]
    for j in range(NZ - 1):
        remote(q.at[z], rz.at[j], zs.at[j], zr.at[j], partner).wait_recv()
        total = total + rz[j]
    sp[...] = total

    def over_x(k, slot):
        return remote(sp.at[lax.rem(x + k + 2 * slot, NX)], rx.at[k - 1, slot], ws.at[k - 1, slot], wr.at[k - 1, slot],
                      at_x(k))

    for k in range(1, NX):
        for slot in range(2):
            over_x(k, slot).start()
    to_right[3].start()
    to_left[3].start()
    for i in range(2):
        left_arrived([i])
        right_arrived([2 + i])
    forward_right[0].start()
    forward_left[0].start()
    accumulate([(left_x, 0, half), (right_x, half, half)])
    for slot in range(2):
        total = sp[lax.rem(x + 2 * slot, NX)]
        for k in range(1, NX):
            over_x(k, slot).wait_recv()
            total = total + rx[k - 1, slot]
        s[core, z, y, slot] = total

    own = s.at[core, z, y]

    def along_z(k):
        return lax.rem(z + NZ - k, NZ)

    def same(piece, send, recv, device):
        return remote(piece, piece, send, recv, device)

    def spread(k):
        piece = s.at[core, along_z(k), y]
        same(piece, gys.at[0, k], gyr.at[0, k], to_up).start()
        same(piece, gys.at[1, k], gyr.at[1, k], to_down).start()

    for k in range(1, NZ):
        same(own, gzs.at[k - 1], gzr.at[k - 1], at_z(lax.rem(z + k, NZ))).start()
    spread(0)

    def from_z(k, carry):
        same(s.at[core, along_z(k), y], gzs.at[k - 1], gzr.at[k - 1], partner).wait_recv()
        spread(k)
        return carry

    lax.fori_loop(1, NZ, from_z, 0)

    def to_partner(r):
        return same(s.at[core, :, lax.rem(y + r, NY)], gcs.at[r], gcr.at[r], partner)

    to_partner(0).start()

    def from_y(first):
        def body(k, carry):
            zz = along_z(k)
            lower, upper = s.at[core, zz, down], s.at[core, zz, up]
            same(lower, gys.at[0, k], gyr.at[0, k], partner).wait_recv()
            same(upper, gys.at[1, k], gyr.at[1, k], partner).wait_recv()
            if first:
                same(lower, ghs.at[k], ghr.at[k], to_up).start()
            else:
                same(upper, ghs.at[k], ghr.at[k], to_down).start()
            return carry
        return body

    lax.fori_loop(0, NZ // 2, from_y(True), 0)
    lax.fori_loop(NZ // 2, NZ, from_y(False), 0)
    to_partner(NY - 1).start()
    to_partner(1).start()

    def from_far(k, carry):
        same(s.at[core, along_z(k), far_y], ghs.at[k], ghr.at[k], partner).wait_recv()
        return carry

    lax.fori_loop(0, NZ, from_far, 0)
    to_partner(2).start()
    left_arrived([2, 3])
    right_arrived([0, 1])
    accumulate([(left_x, half, half), (right_x, 0, half)])
    for r in range(NY):
        same(s.at[other, :, lax.rem(y + r, NY)], gcs.at[r], gcr.at[r], partner).wait_recv()

    def two_terms(dst, slot):
        for m in range(2):
            for zz in range(NZ):
                for yy in range(NY):
                    d0 = (zz * NY + yy) * 128
                    high, low = split(s[m, zz, yy, slot])
                    dst[m * 64:m * 64 + 32, d0:d0 + 128] = high
                    dst[m * 64 + 32:m * 64 + 64, d0:d0 + 128] = low

    two_terms(sf, 1)
    u = dot(sf[...], a[x], NT)
    for m in range(2):
        us[m * RANK:(m + 1) * RANK, :] = u[m * 64:m * 64 + 32] + u[m * 64 + 32:m * 64 + 64]
    to_far = remote(us, uf, us_sem.at[0], ur_sem.at[0], at_x(2))
    to_far.start()
    forward_right[1].start()
    forward_left[1].start()
    two_terms(sb, 0)

    right = []
    for m in range(2):
        both = dot(sb[m * 64:m * 64 + 64, :], e[m])
        right.append(both[:RANK] + both[RANK:])

    def add_right(slot, m, um):
        tok = pl.ds(pl.multiple_of(slot * tokens, tokens), tokens)
        both = dot(jnp.concatenate(split(um), axis=0), c[m, tok, :])
        right[m] = right[m] + both[:RANK] + both[RANK:]

    for slot in (x, left_x, right_x):
        u = dot(sb[...], a[slot], NT)
        for m in range(2):
            add_right(slot, m, u[m * 64:m * 64 + 32] + u[m * 64 + 32:m * 64 + 64])
    to_far.wait_recv()
    for m in range(2):
        add_right(far_x, m, uf[m * RANK:(m + 1) * RANK, :])

    group = t.shape[2]
    per_row = kv // 128

    def piece(i):
        return i // group, i % group

    for m in range(2):
        for i in range(NZ * group):
            rr, kk = i // per_row, i % per_row
            t[(m,) + piece(i)] = right[m][rr * 8:rr * 8 + 8, kk * 128:kk * 128 + 128]
    for i, (d, k) in enumerate(plane):
        zk, ck = lax.rem(z + k, NZ), (core, other)[d]
        remote(t.at[ck, zk], ta.at[i], tas.at[i], tar.at[i], at_zc(zk, ck)).start()
    inverse = []
    for m in range(2):
        both = dot(sb[m * 64:m * 64 + 64, :], sb[m * 64:m * 64 + 64, :], NT)
        inverse.append(inverse_factor(
            both[:RANK, :RANK] + both[:RANK, RANK:] + both[RANK:, :RANK] + both[RANK:, RANK:]))
    total = t[core, z]
    for i in range(len(plane)):
        remote(t.at[core, z], ta.at[i], tas.at[i], tar.at[i], partner).wait_recv()
        total = total + ta[i]
    t2[...] = total
    for k in range(1, NY):
        remote(t2, ty.at[k - 1], tys.at[k - 1], tyr.at[k - 1], at_y(k)).start()
    for k in range(1, NY):
        remote(t2, ty.at[k - 1], tys.at[k - 1], tyr.at[k - 1], partner).wait_recv()
        total = total + ty[k - 1]
    tf[core, z] = total
    own_t = tf.at[core, z]
    for i, (d, k) in enumerate(plane):
        remote(own_t, own_t, tgs.at[i], tgr.at[i], at_zc(lax.rem(z + k, NZ), (core, other)[d])).start()
    for m in range(2):
        high, low = split(inverse[m])
        pair = jnp.concatenate([high, low], axis=0)
        for i in range(width // step):
            at = pl.ds(i * step, step)
            both = dot(pair, sb[m * 64:m * 64 + 32, at])
            lt = both[:RANK] + both[RANK:] + dot(high, sb[m * 64 + 32:m * 64 + 64, at])
            left[m, :, at] = lt
            lh, ll = split(lt)
            stack[m * 96:m * 96 + 96, at] = jnp.concatenate([lh, ll, lh], axis=0)
    store_left = pltpu.make_async_copy(left, left_hbm, lsem.at[4])
    store_left.start()
    for i, (d, k) in enumerate(plane):
        got = tf.at[(core, other)[d], lax.rem(z + NZ - k, NZ)]
        remote(got, got, tgs.at[i], tgr.at[i], partner).wait_recv()

    means = []
    for m in range(2):
        tt = jnp.concatenate(
            [jnp.concatenate([tf[(m,) + piece(rr * per_row + kk)] for kk in range(per_row)], axis=1)
             for rr in range(RANK // 8)], axis=0)
        wh, wl = split(inverse[m])
        th, tl = split(tt)
        both = dot(jnp.concatenate([wh, wl], axis=0), th)
        mean = (both[:RANK] + both[RANK:] + dot(wh, tl)) * (1.0 / ndp)
        mean_ref[m] = mean
        mh, ml = split(mean)
        means.append(jnp.concatenate([mh, mh, ml], axis=0))

    def subtract(i, carry):
        at = pl.ds(pl.multiple_of(i * step, step), step)
        for m in range(2):
            mem[m, at, :] = mem[m, at, :] - dot(stack[m * 96:m * 96 + 96, at], means[m], TN)
        return carry

    lax.fori_loop(0, width // step, subtract, 0)

    far_arrived()
    far_parts = [(far_x, 0, tokens)]
    cc_far = cotangents(far_parts)

    def store_new(i):
        at = pl.ds(pl.multiple_of(i * step, step), step)
        return pltpu.make_async_copy(new.at[:, at], new_hbm.at[:, at], out_sem.at[i])

    def finish(i, carry):
        at = pl.ds(pl.multiple_of(i * step, step), step)
        g = product(far_parts, cc_far, at)
        for m in range(2):
            new[m, at, :] = (mem[m, at, :] + g[:, m * kv:(m + 1) * kv]).astype(BF)
        store_new(i).start()
        return carry

    lax.fori_loop(0, width // step, finish, 0)

    for copy in v_copies + to_right + to_left + forward_right + forward_left:
        copy.wait_send()

    def sent(j, carry):
        remote(p.at[other, j], rc.at[j], cs.at[j], cr.at[j], partner).wait_send()
        for i in range(2):
            remote(fy.at[i, j], fy.at[i, j], fs.at[i, j], fr.at[i, j], partner).wait_send()
            remote(p.at[core, j, y], ry.at[i, j], ys.at[i, j], yr.at[i, j], partner).wait_send()
        return carry

    lax.fori_loop(0, NZ, sent, 0)
    for j in range(NZ - 1):
        remote(q.at[j], rz.at[j], zs.at[j], zr.at[j], partner).wait_send()
        same(own, gzs.at[j], gzr.at[j], partner).wait_send()
    for k in range(1, NX):
        for slot in range(2):
            over_x(k, slot).wait_send()

    def sent_s(k, carry):
        same(own, gys.at[0, k], gyr.at[0, k], partner).wait_send()
        same(own, gys.at[1, k], gyr.at[1, k], partner).wait_send()
        same(own, ghs.at[k], ghr.at[k], partner).wait_send()
        return carry

    lax.fori_loop(0, NZ, sent_s, 0)
    for r in range(NY):
        to_partner(r).wait_send()
    to_far.wait_send()
    for i in range(len(plane)):
        remote(t2, ta.at[i], tas.at[i], tar.at[i], partner).wait_send()
        remote(own_t, own_t, tgs.at[i], tgr.at[i], partner).wait_send()
    for k in range(NY - 1):
        remote(t2, ty.at[k], tys.at[k], tyr.at[k], partner).wait_send()
    store_left.wait()

    def stored(i, carry):
        store_new(i).wait()
        return carry

    lax.fori_loop(0, width // step, stored, 0)


def hand_over(parts, new_hbm, left_hbm, mean_ref, new_out, left_out, mean_out, new, left, load_sem, store_sem):
    rows = new_hbm.shape[1] // parts
    at = [(m, pl.ds(i * rows, rows)) for m in range(2) for i in range(parts)]
    moves = [(new_hbm.at[w], new.at[w], new_out.at[w]) for w in at]
    moves += [(left_hbm.at[m], left.at[m], left_out.at[m]) for m in range(2)]
    loads = [pltpu.make_async_copy(src, mid, load_sem.at[i]) for i, (src, mid, dst) in enumerate(moves)]
    stores = [pltpu.make_async_copy(mid, dst, store_sem.at[i]) for i, (src, mid, dst) in enumerate(moves)]
    flight = 4
    for load in loads[:flight]:
        load.start()
    mean_out[...] = mean_ref[...]
    for i in range(len(moves)):
        loads[i].wait()
        if i + flight < len(moves):
            loads[i + flight].start()
        stores[i].start()
    for store in stores:
        store.wait()


def shards(NY, NZ, activations, cotangent, error_memory, right_factor):
    tokens, width = activations.shape
    kv = cotangent.shape[2]
    error_memory = error_memory[:, 0]
    group = RANK * kv // (8 * 128 * NZ)
    dma = pltpu.SemaphoreType.DMA
    any_spec = pl.BlockSpec(memory_space=pl.ANY)
    new_error, left, mean = pl.pallas_call(
        functools.partial(fused, NY, NZ),
        out_shape=(
            jax.ShapeDtypeStruct((2, width, kv), BF),
            jax.ShapeDtypeStruct((2, RANK, width), F32),
            jax.ShapeDtypeStruct((2, RANK, kv), F32),
        ),
        in_specs=[any_spec] * 4,
        out_specs=(any_spec, any_spec, pl.BlockSpec(memory_space=pltpu.VMEM)),
        scratch_shapes=[
            pltpu.VMEM((NX, tokens, width), BF),
            pltpu.VMEM((2, NX * tokens, kv), BF),
            pltpu.VMEM((2, width, kv), BF),
            pltpu.VMEM((2, RANK, kv), F32),
            pltpu.VMEM((NX, 2 * RANK, tokens), F32),
            pltpu.VMEM((NX, 2 * RANK, tokens), F32),
            pltpu.VMEM((4 * NX * RANK, tokens), BF),
            pltpu.VMEM((2, 2 * RANK, kv), BF),
            pltpu.VMEM((2, NZ, NY, RANK, 128), F32),
            pltpu.VMEM((2, NZ, NY, NX, RANK, 128), F32),
            pltpu.VMEM((NZ, NY, NX, RANK, 128), F32),
            pltpu.VMEM((2, NZ, NX // 2, RANK, 128), F32),
            pltpu.VMEM((2, NZ, NX, RANK, 128), F32),
            pltpu.VMEM((NZ, NX, RANK, 128), F32),
            pltpu.VMEM((NZ - 1, NX, RANK, 128), F32),
            pltpu.VMEM((NX, RANK, 128), F32),
            pltpu.VMEM((NX - 1, 2, RANK, 128), F32),
            pltpu.VMEM((2, NZ, NY, 2, RANK, 128), F32),
            pltpu.VMEM((4 * RANK, width), BF),
            pltpu.VMEM((4 * RANK, width), BF),
            pltpu.VMEM((2 * RANK, tokens), F32),
            pltpu.VMEM((2 * RANK, tokens), F32),
            pltpu.VMEM((2, RANK, width), F32),
            pltpu.VMEM((6 * RANK, width), BF),
            pltpu.VMEM((2, width, kv), F32),
            pltpu.VMEM((2, width, kv), BF),
            pltpu.VMEM((2, NZ, group, 8, 128), F32),
            pltpu.VMEM((2 * NZ - 1, group, 8, 128), F32),
            pltpu.VMEM((group, 8, 128), F32),
            pltpu.VMEM((NY - 1, group, 8, 128), F32),
            pltpu.VMEM((2, NZ, group, 8, 128), F32),
            dma((6,)),
            dma((NX - 1,)), dma((NX - 1,)),
            dma((12,)), dma((12,)),
            dma((NZ,)), dma((NZ,)),
            dma((2, NZ)), dma((2, NZ)),
            dma((2, NZ)), dma((2, NZ)),
            dma((NZ - 1,)), dma((NZ - 1,)),
            dma((NX - 1, 2)), dma((NX - 1, 2)),
            dma((NZ - 1,)), dma((NZ - 1,)),
            dma((2, NZ)), dma((2, NZ)),
            dma((NZ,)), dma((NZ,)),
            dma((NY,)), dma((NY,)),
            dma((1,)), dma((1,)),
            dma((2 * NZ - 1,)), dma((2 * NZ - 1,)),
            dma((NY - 1,)), dma((NY - 1,)),
            dma((2 * NZ - 1,)), dma((2 * NZ - 1,)),
            dma((max(1, width // 512),)),
        ],
        compiler_params=pltpu.CompilerParams(
            collective_id=0, has_side_effects=True, vmem_limit_bytes=56 * 1024 * 1024),
    )(activations, cotangent, error_memory, jnp.swapaxes(right_factor, 1, 2))

    parts = 4
    vmem_spec = pl.BlockSpec(memory_space=pltpu.VMEM)
    new_error, left, mean = pl.pallas_call(
        functools.partial(hand_over, parts),
        out_shape=(
            jax.ShapeDtypeStruct((2, width, kv), BF),
            jax.ShapeDtypeStruct((2, RANK, width), F32),
            jax.ShapeDtypeStruct((2, RANK, kv), F32),
        ),
        in_specs=[any_spec, any_spec, vmem_spec],
        out_specs=(any_spec, any_spec, vmem_spec),
        scratch_shapes=[
            pltpu.VMEM((2, width, kv), BF),
            pltpu.VMEM((2, RANK, width), F32),
            dma((2 * parts + 2,)),
            dma((2 * parts + 2,)),
        ],
        compiler_params=pltpu.CompilerParams(vmem_limit_bytes=56 * 1024 * 1024),
    )(new_error, left, mean)
    return (new_error[:, None], jnp.swapaxes(left, 1, 2)[:, None], jnp.swapaxes(mean, 1, 2))


def build(mesh, NY, NZ):
    return jax.shard_map(
        functools.partial(shards, NY, NZ),
        mesh=mesh,
        in_specs=(
            P(("dp", "tensor"), None),
            P(None, "dp", "tensor"),
            P(None, "dp", None, "tensor"),
            P(None, "tensor", None),
        ),
        out_specs=(
            P(None, "dp", None, "tensor"),
            P(None, "tensor", None, None),
            P(None, "tensor", None),
        ),
        check_vma=False,
    )


def solution(mesh):
    return build(mesh, 4, mesh.shape["dp"] // 8)
```

profile of v0, /device:TPU:1, one launch (start us, length us, event | category | flops | bytes accessed | tf_op | source)
XLA Modules:
  0.0 107.1 jit_solution(8794946512857347003)
XLA Ops:
  0.6 99.4 %shard_map.67 = (bf16[2,4096,256]{2,1,0:T(8,128)(2,1)}, f32[2,32,4096]{2,1,0:T(8,128)}, f32[2,32,256]{2,1,0:T(8,128)}) custom-call(bf16[256,4096]{1,0:T(8,128)(2,1)} %a_hbm.1, bf16[2,1024,256]{2,1,0:T(8,128)(2,1)} %c_hbm.1, bf16[2,4096,256]{2,1,0:T(8,128)(2,1)} %bitcast.11, f32[2,32,256]{2,1,0:T(8,128)} %bitcast.12), custom_call_target="tpu_custom_call" | custom-call | tf_op jit(solution)/shard_map/pallas_call | solution.py:545
  100.1 7.0 %shard_map.68 = (bf16[2,4096,256]{2,1,0:T(8,128)(2,1)}, f32[2,32,4096]{2,1,0:T(8,128)}, f32[2,32,256]{2,1,0:T(8,128)}) custom-call(bf16[2,4096,256]{2,1,0:T(8,128)(2,1)} %get-tuple-element.9.new_hbm, f32[2,32,4096]{2,1,0:T(8,128)} %get-tuple-element.10.left_hbm, f32[2,32,256]{2,1,0:T(8,128)} %get-tuple-element.11.mean_ref), custom_call_target="tpu_custom_call" | custom-call | tf_op jit(solution)/shard_map/pallas_call | solution.py:610
where the time goes:
time: 107 us
  Pallas kernels  106 us (99%)
    pallas_call x1, Pallas kernels, shards(): pl.pallas_call(functools.partial(fused, NY, NZ), out_shape=(jax.ShapeDtyp...  99.4 us
    pallas_call x1, Pallas kernels, shards(): pl.pallas_call(functools.partial(hand_over, parts), out_shape=(jax.ShapeD...  7 us

commit v1 on v0

--- a/solution.py
+++ b/solution.py
@@ -27,25 +27,34 @@
     return lax.dot_general(a, b, dims, preferred_element_type=F32)
 
 
-def inverse_factor(gram):
-    rows = lax.broadcasted_iota(jnp.int32, (RANK, 2 * RANK), 0)
-    cols = lax.broadcasted_iota(jnp.int32, (RANK, 2 * RANK), 1)
-    eye = jnp.where(cols == rows + RANK, 1.0, 0.0).astype(F32)
-    wide = jnp.concatenate([gram, jnp.zeros((RANK, RANK), F32)], axis=1) + eye
-    index = rows[:, :1]
-    pivots = jnp.ones((RANK, 1), F32)
-    for j in range(RANK):
+def eliminate(state, first, last):
+    wide, pivots = state
+    index = lax.broadcasted_iota(jnp.int32, (RANK, 1), 0)
+    for j in range(first, last):
         row = wide[j:j + 1, :]
         pivot = wide[j:j + 1, j:j + 1]
         column = wide[:, j:j + 1]
         factor = jnp.where(index > j, column * (1.0 / pivot), 0.0)
         pivots = jnp.where(index == j, pivot, pivots)
         wide = wide - factor * row
+    return wide, pivots
+
+
+def elimination(gram):
+    rows = lax.broadcasted_iota(jnp.int32, (RANK, 2 * RANK), 0)
+    cols = lax.broadcasted_iota(jnp.int32, (RANK, 2 * RANK), 1)
+    eye = jnp.where(cols == rows + RANK, 1.0, 0.0).astype(F32)
+    wide = jnp.concatenate([gram, jnp.zeros((RANK, RANK), F32)], axis=1) + eye
+    return wide, jnp.ones((RANK, 1), F32)
+
+
+def inverse_factor(state):
+    wide, pivots = state
     return wide[:, RANK:] * (1.0 / jnp.sqrt(pivots))
 
 
-def fused(NY, NZ, a_hbm, c_hbm, e_hbm, rt_hbm, new_hbm, left_hbm, mean_ref,
-          a, c, e, rt, v, vall, vl, rb, pe, p, rc, fy, ry, q, rz, sp, rx, s, sb, sf, us, uf, left, stack, mem, new,
+def fused(NY, NZ, a_hbm, c_hbm, e_hbm, rt_hbm, new_hbm, left_hbm, mean_hbm,
+          a, c, e, rt, v, vall, vl, rb, pe, p, rc, fy, ry, q, rz, sp, rx, s, sb, sf, us, uf, left, stack, mem, new, means_f32,
           t, ta, t2, ty, tf,
           lsem, vs, vr, xs, xr, cs, cr, fs, fr, ys, yr, zs, zr, ws, wr, gzs, gzr, gys, gyr, ghs, ghr, gcs, gcr,
           us_sem, ur_sem, tas, tar, tys, tyr, tgs, tgr, out_sem):
@@ -382,6 +391,11 @@
         u = dot(sb[...], a[slot], NT)
         for m in range(2):
             add_right(slot, m, u[m * 64:m * 64 + 32] + u[m * 64 + 32:m * 64 + 64])
+    states = []
+    for m in range(2):
+        both = dot(sb[m * 64:m * 64 + 64, :], sb[m * 64:m * 64 + 64, :], NT)
+        states.append(elimination(
+            both[:RANK, :RANK] + both[:RANK, RANK:] + both[RANK:, :RANK] + both[RANK:, RANK:]))
     to_far.wait_recv()
     for m in range(2):
         add_right(far_x, m, uf[m * RANK:(m + 1) * RANK, :])
@@ -399,11 +413,7 @@
     for i, (d, k) in enumerate(plane):
         zk, ck = lax.rem(z + k, NZ), (core, other)[d]
         remote(t.at[ck, zk], ta.at[i], tas.at[i], tar.at[i], at_zc(zk, ck)).start()
-    inverse = []
-    for m in range(2):
-        both = dot(sb[m * 64:m * 64 + 64, :], sb[m * 64:m * 64 + 64, :], NT)
-        inverse.append(inverse_factor(
-            both[:RANK, :RANK] + both[:RANK, RANK:] + both[RANK:, :RANK] + both[RANK:, RANK:]))
+    states = [eliminate(state, 0, 11) for state in states]
     total = t[core, z]
     for i in range(len(plane)):
         remote(t.at[core, z], ta.at[i], tas.at[i], tar.at[i], partner).wait_recv()
@@ -411,6 +421,7 @@
     t2[...] = total
     for k in range(1, NY):
         remote(t2, ty.at[k - 1], tys.at[k - 1], tyr.at[k - 1], at_y(k)).start()
+    states = [eliminate(state, 11, 22) for state in states]
     for k in range(1, NY):
         remote(t2, ty.at[k - 1], tys.at[k - 1], tyr.at[k - 1], partner).wait_recv()
         total = total + ty[k - 1]
@@ -418,6 +429,7 @@
     own_t = tf.at[core, z]
     for i, (d, k) in enumerate(plane):
         remote(own_t, own_t, tgs.at[i], tgr.at[i], at_zc(lax.rem(z + k, NZ), (core, other)[d])).start()
+    inverse = [inverse_factor(eliminate(state, 22, RANK)) for state in states]
     for m in range(2):
         high, low = split(inverse[m])
         pair = jnp.concatenate([high, low], axis=0)
@@ -443,9 +455,11 @@
         th, tl = split(tt)
         both = dot(jnp.concatenate([wh, wl], axis=0), th)
         mean = (both[:RANK] + both[RANK:] + dot(wh, tl)) * (1.0 / ndp)
-        mean_ref[m] = mean
+        means_f32[m] = mean
         mh, ml = split(mean)
         means.append(jnp.concatenate([mh, mh, ml], axis=0))
+    store_mean = pltpu.make_async_copy(means_f32, mean_hbm, lsem.at[5])
+    store_mean.start()
 
     def subtract(i, carry):
         at = pl.ds(pl.multiple_of(i * step, step), step)
@@ -507,6 +521,7 @@
     for k in range(NY - 1):
         remote(t2, ty.at[k], tys.at[k], tyr.at[k], partner).wait_send()
     store_left.wait()
+    store_mean.wait()
 
     def stored(i, carry):
         store_new(i).wait()
@@ -515,22 +530,19 @@
     lax.fori_loop(0, width // step, stored, 0)
 
 
-def hand_over(parts, new_hbm, left_hbm, mean_ref, new_out, left_out, mean_out, new, left, load_sem, store_sem):
+def hand_over(parts, new_hbm, left_hbm, mean_hbm, new_out, left_out, mean_out, new, left, mean, load_sem, store_sem):
     rows = new_hbm.shape[1] // parts
     at = [(m, pl.ds(i * rows, rows)) for m in range(2) for i in range(parts)]
     moves = [(new_hbm.at[w], new.at[w], new_out.at[w]) for w in at]
     moves += [(left_hbm.at[m], left.at[m], left_out.at[m]) for m in range(2)]
+    moves += [(mean_hbm, mean, mean_out)]
     loads = [pltpu.make_async_copy(src, mid, load_sem.at[i]) for i, (src, mid, dst) in enumerate(moves)]
     stores = [pltpu.make_async_copy(mid, dst, store_sem.at[i]) for i, (src, mid, dst) in enumerate(moves)]
-    flight = 4
-    for load in loads[:flight]:
+    for load in loads:
         load.start()
-    mean_out[...] = mean_ref[...]
-    for i in range(len(moves)):
-        loads[i].wait()
-        if i + flight < len(moves):
-            loads[i + flight].start()
-        stores[i].start()
+    for load, store in zip(loads, stores):
+        load.wait()
+        store.start()
     for store in stores:
         store.wait()
 
@@ -550,7 +562,7 @@
             jax.ShapeDtypeStruct((2, RANK, kv), F32),
         ),
         in_specs=[any_spec] * 4,
-        out_specs=(any_spec, any_spec, pl.BlockSpec(memory_space=pltpu.VMEM)),
+        out_specs=(any_spec,) * 3,
         scratch_shapes=[
             pltpu.VMEM((NX, tokens, width), BF),
             pltpu.VMEM((2, NX * tokens, kv), BF),
@@ -578,6 +590,7 @@
             pltpu.VMEM((6 * RANK, width), BF),
             pltpu.VMEM((2, width, kv), F32),
             pltpu.VMEM((2, width, kv), BF),
+            pltpu.VMEM((2, RANK, kv), F32),
             pltpu.VMEM((2, NZ, group, 8, 128), F32),
             pltpu.VMEM((2 * NZ - 1, group, 8, 128), F32),
             pltpu.VMEM((group, 8, 128), F32),
@@ -606,7 +619,6 @@
     )(activations, cotangent, error_memory, jnp.swapaxes(right_factor, 1, 2))
 
     parts = 4
-    vmem_spec = pl.BlockSpec(memory_space=pltpu.VMEM)
     new_error, left, mean = pl.pallas_call(
         functools.partial(hand_over, parts),
         out_shape=(
@@ -614,13 +626,14 @@
             jax.ShapeDtypeStruct((2, RANK, width), F32),
             jax.ShapeDtypeStruct((2, RANK, kv), F32),
         ),
-        in_specs=[any_spec, any_spec, vmem_spec],
-        out_specs=(any_spec, any_spec, vmem_spec),
+        in_specs=[any_spec] * 3,
+        out_specs=(any_spec,) * 3,
         scratch_shapes=[
             pltpu.VMEM((2, width, kv), BF),
             pltpu.VMEM((2, RANK, width), F32),
-            dma((2 * parts + 2,)),
-            dma((2 * parts + 2,)),
+            pltpu.VMEM((2, RANK, kv), F32),
+            dma((2 * parts + 3,)),
+            dma((2 * parts + 3,)),
         ],
         compiler_params=pltpu.CompilerParams(vmem_limit_bytes=56 * 1024 * 1024),
     )(new_error, left, mean)

time: 107 us -> 106 us (level)
    pallas_call x1, Pallas kernels: 7 us -> 4.73 us  [shards(): pl.pallas_call(functools.partial(hand_over, parts), out_shape=(jax.ShapeD...]
    pallas_call x1, Pallas kernels: 99.4 us -> 101 us  [shards(): pl.pallas_call(functools.partial(fused, NY, NZ), out_shape=(jax.ShapeDtyp...]
where the time goes in v1:
time: 106 us
  Pallas kernels  105 us (99%)
    pallas_call x1, Pallas kernels, shards(): pl.pallas_call(functools.partial(fused, NY, NZ), out_shape=(jax.ShapeDtyp...  101 us
    pallas_call x1, Pallas kernels, shards(): pl.pallas_call(functools.partial(hand_over, parts), out_shape=(jax.ShapeD...  4.73 us

profile of v1, /device:TPU:1, one launch (start us, length us, event | category | flops | bytes accessed | tf_op | source)
XLA Modules:
  0.0 105.9 jit_solution(6228090405105319244)
XLA Ops:
  0.6 100.6 %shard_map.67 = (bf16[2,4096,256]{2,1,0:T(8,128)(2,1)}, f32[2,32,4096]{2,1,0:T(8,128)}, f32[2,32,256]{2,1,0:T(8,128)}) custom-call(bf16[256,4096]{1,0:T(8,128)(2,1)} %a_hbm.1, bf16[2,1024,256]{2,1,0:T(8,128)(2,1)} %c_hbm.1, bf16[2,4096,256]{2,1,0:T(8,128)(2,1)} %bitcast.11, f32[2,32,256]{2,1,0:T(8,128)} %bitcast.12), custom_call_target="tpu_custom_call" | custom-call | tf_op jit(solution)/shard_map/pallas_call | solution.py:557
  101.2 4.7 %shard_map.68 = (bf16[2,4096,256]{2,1,0:T(8,128)(2,1)}, f32[2,32,4096]{2,1,0:T(8,128)}, f32[2,32,256]{2,1,0:T(8,128)}) custom-call(bf16[2,4096,256]{2,1,0:T(8,128)(2,1)} %get-tuple-element.9.new_hbm, f32[2,32,4096]{2,1,0:T(8,128)} %get-tuple-element.10.left_hbm, f32[2,32,256]{2,1,0:T(8,128)} %get-tuple-element.11.mean_hbm), custom_call_target="tpu_custom_call" | custom-call | tf_op jit(solution)/shard_map/pallas_call | solution.py:622

commit v2 on v1

--- a/solution.py
+++ b/solution.py
@@ -442,6 +442,8 @@
             stack[m * 96:m * 96 + 96, at] = jnp.concatenate([lh, ll, lh], axis=0)
     store_left = pltpu.make_async_copy(left, left_hbm, lsem.at[4])
     store_left.start()
+    far_arrived()
+    accumulate([(far_x, 0, tokens)])
     for i, (d, k) in enumerate(plane):
         got = tf.at[(core, other)[d], lax.rem(z + NZ - k, NZ)]
         remote(got, got, tgs.at[i], tgr.at[i], partner).wait_recv()
@@ -461,27 +463,15 @@
     store_mean = pltpu.make_async_copy(means_f32, mean_hbm, lsem.at[5])
     store_mean.start()
 
-    def subtract(i, carry):
-        at = pl.ds(pl.multiple_of(i * step, step), step)
-        for m in range(2):
-            mem[m, at, :] = mem[m, at, :] - dot(stack[m * 96:m * 96 + 96, at], means[m], TN)
-        return carry
-
-    lax.fori_loop(0, width // step, subtract, 0)
-
-    far_arrived()
-    far_parts = [(far_x, 0, tokens)]
-    cc_far = cotangents(far_parts)
-
     def store_new(i):
         at = pl.ds(pl.multiple_of(i * step, step), step)
         return pltpu.make_async_copy(new.at[:, at], new_hbm.at[:, at], out_sem.at[i])
 
     def finish(i, carry):
         at = pl.ds(pl.multiple_of(i * step, step), step)
-        g = product(far_parts, cc_far, at)
         for m in range(2):
-            new[m, at, :] = (mem[m, at, :] + g[:, m * kv:(m + 1) * kv]).astype(BF)
+            approx = dot(stack[m * 96:m * 96 + 96, at], means[m], TN)
+            new[m, at, :] = (mem[m, at, :] - approx).astype(BF)
         store_new(i).start()
         return carry
 

time: 106 us -> 103 us (0.972)
  Pallas kernels: 105 us -> 103 us
    pallas_call x1, Pallas kernels: 101 us -> 97.9 us  [shards(): pl.pallas_call(functools.partial(fused, NY, NZ), out_shape=(jax.ShapeDtyp...]
where the time goes in v2:
time: 103 us
  Pallas kernels  103 us (100%)
    pallas_call x1, Pallas kernels, shards(): pl.pallas_call(functools.partial(fused, NY, NZ), out_shape=(jax.ShapeDtyp...  97.9 us
    pallas_call x1, Pallas kernels, shards(): pl.pallas_call(functools.partial(hand_over, parts), out_shape=(jax.ShapeD...  4.73 us

profile of v2, /device:TPU:1, one launch (start us, length us, event | category | flops | bytes accessed | tf_op | source)
XLA Modules:
  0.0 103.2 jit_solution(9410091178503564547)
XLA Ops:
  0.6 97.9 %shard_map.67 = (bf16[2,4096,256]{2,1,0:T(8,128)(2,1)}, f32[2,32,4096]{2,1,0:T(8,128)}, f32[2,32,256]{2,1,0:T(8,128)}) custom-call(bf16[256,4096]{1,0:T(8,128)(2,1)} %a_hbm.1, bf16[2,1024,256]{2,1,0:T(8,128)(2,1)} %c_hbm.1, bf16[2,4096,256]{2,1,0:T(8,128)(2,1)} %bitcast.11, f32[2,32,256]{2,1,0:T(8,128)} %bitcast.12), custom_call_target="tpu_custom_call" | custom-call | tf_op jit(solution)/shard_map/pallas_call | solution.py:547
  98.5 4.7 %shard_map.68 = (bf16[2,4096,256]{2,1,0:T(8,128)(2,1)}, f32[2,32,4096]{2,1,0:T(8,128)}, f32[2,32,256]{2,1,0:T(8,128)}) custom-call(bf16[2,4096,256]{2,1,0:T(8,128)(2,1)} %get-tuple-element.9.new_hbm, f32[2,32,4096]{2,1,0:T(8,128)} %get-tuple-element.10.left_hbm, f32[2,32,256]{2,1,0:T(8,128)} %get-tuple-element.11.mean_hbm), custom_call_target="tpu_custom_call" | custom-call | tf_op jit(solution)/shard_map/pallas_call | solution.py:612

commit v3 on v2

--- a/solution.py
+++ b/solution.py
@@ -352,9 +352,6 @@
 
     lax.fori_loop(0, NZ, from_far, 0)
     to_partner(2).start()
-    left_arrived([2, 3])
-    right_arrived([0, 1])
-    accumulate([(left_x, half, half), (right_x, 0, half)])
     for r in range(NY):
         same(s.at[other, :, lax.rem(y + r, NY)], gcs.at[r], gcr.at[r], partner).wait_recv()
 
@@ -387,6 +384,8 @@
         both = dot(jnp.concatenate(split(um), axis=0), c[m, tok, :])
         right[m] = right[m] + both[:RANK] + both[RANK:]
 
+    left_arrived([2, 3])
+    right_arrived([0, 1])
     for slot in (x, left_x, right_x):
         u = dot(sb[...], a[slot], NT)
         for m in range(2):
@@ -414,6 +413,7 @@
         zk, ck = lax.rem(z + k, NZ), (core, other)[d]
         remote(t.at[ck, zk], ta.at[i], tas.at[i], tar.at[i], at_zc(zk, ck)).start()
     states = [eliminate(state, 0, 11) for state in states]
+    accumulate([(left_x, half, half), (right_x, 0, half)])
     total = t[core, z]
     for i in range(len(plane)):
         remote(t.at[core, z], ta.at[i], tas.at[i], tar.at[i], partner).wait_recv()

time: 103 us -> 103 us (level)
  no operation moved by 1% of the time
where the time goes in v3:
time: 103 us
  Pallas kernels  103 us (100%)
    pallas_call x1, Pallas kernels, shards(): pl.pallas_call(functools.partial(fused, NY, NZ), out_shape=(jax.ShapeDtyp...  98 us
    pallas_call x1, Pallas kernels, shards(): pl.pallas_call(functools.partial(hand_over, parts), out_shape=(jax.ShapeD...  4.73 us

profile of v3, /device:TPU:1, one launch (start us, length us, event | category | flops | bytes accessed | tf_op | source)
XLA Modules:
  0.0 103.4 jit_solution(8183517929330003583)
XLA Ops:
  0.6 98.0 %shard_map.67 = (bf16[2,4096,256]{2,1,0:T(8,128)(2,1)}, f32[2,32,4096]{2,1,0:T(8,128)}, f32[2,32,256]{2,1,0:T(8,128)}) custom-call(bf16[256,4096]{1,0:T(8,128)(2,1)} %a_hbm.1, bf16[2,1024,256]{2,1,0:T(8,128)(2,1)} %c_hbm.1, bf16[2,4096,256]{2,1,0:T(8,128)(2,1)} %bitcast.11, f32[2,32,256]{2,1,0:T(8,128)} %bitcast.12), custom_call_target="tpu_custom_call" | custom-call | tf_op jit(solution)/shard_map/pallas_call | solution.py:547
  98.6 4.7 %shard_map.68 = (bf16[2,4096,256]{2,1,0:T(8,128)(2,1)}, f32[2,32,4096]{2,1,0:T(8,128)}, f32[2,32,256]{2,1,0:T(8,128)}) custom-call(bf16[2,4096,256]{2,1,0:T(8,128)(2,1)} %get-tuple-element.9.new_hbm, f32[2,32,4096]{2,1,0:T(8,128)} %get-tuple-element.10.left_hbm, f32[2,32,256]{2,1,0:T(8,128)} %get-tuple-element.11.mean_hbm), custom_call_target="tpu_custom_call" | custom-call | tf_op jit(solution)/shard_map/pallas_call | solution.py:612
